TPU v7x, 256 devices: a whole 4x4x8 slice. The times are simulated.
256 devices in a mesh: gz: 32 (over z_hi, y, core), gx: 8 (over x, z_lo).
Axes of the slice: x: 4, y: 4, z: 8 (z_hi: 4, z_lo: 2; z = z_hi * 2 + z_lo), core: 2. Of those that a mesh axis runs over, the one named last changes fastest.
Arguments:
- density: float32 [4096, 4096], P('gz', 'gx'), may hold values from -6 to 6
- ztaps: float32 [32, 512], replicated, may hold values from -0.25 to 0.25
- xtaps: float32 [32, 256], replicated, may hold values from -0.0625 to 0.0625
Outputs:
- wake: float32 [4096, 4096], P('gz', 'gx')
All inputs are finite; a program needn't handle non-finite values.
Results may differ from a plain program's by a relative error of at most 0.0001.
Values sent between devices are 32-bit elements; how exact they have to be, the bound alone decides.
A program may use at most 192 MiB of HBM per device.

v0:
```python
import jax
import jax.numpy as jnp
import ml_dtypes
import numpy as np
from jax import lax
from jax.experimental import pallas as pl
from jax.experimental.pallas import tpu as pltpu
from jax.sharding import PartitionSpec as P

MESH = pl.DeviceIdType.MESH
F32, BF16 = jnp.float32, jnp.bfloat16
LZ, LX = 768, 512
NORM = 4.0 / (LZ * LX)


def split_np(matrix):
    high = matrix.astype(ml_dtypes.bfloat16)
    low = (matrix - high.astype(np.float64)).astype(ml_dtypes.bfloat16)
    return np.stack([high, low])


def constants():
    freq = np.arange(LZ // 2)
    angle = 2 * np.pi * np.outer(freq + 0.5, np.arange(LZ)) / LZ
    both = np.stack([np.cos(angle).reshape(3, 128, LZ), -np.sin(angle).reshape(3, 128, LZ)], axis=1)
    fz = both.reshape(LZ, LZ)
    angle = 2 * np.pi * np.outer(np.arange(LX), np.arange(LX // 2) + 0.5) / LX
    fx = np.concatenate([np.cos(angle), -np.sin(angle)], axis=1)
    return split_np(fz), split_np(fz[:, :256].T), split_np(fx[:256]), split_np(fx.T)


def dot(a, b, dims=((1,), (0,))):
    return lax.dot_general(a, b, (dims, ((), ())), preferred_element_type=F32)


def dot3(ah, al, bh, bl, dims=((1,), (0,))):
    return dot(ah, bh, dims) + dot(ah, bl, dims) + dot(al, bh, dims)


def split(value):
    high = value.astype(BF16)
    return high, (value - high.astype(F32)).astype(BF16)


def kernel(
    dens, zt_ref, xt_ref, fz_hbm, iz_hbm, fx_hbm, ix_hbm, out,
    win, fz, iz, fx, ix, acc, khat, zt, what, wake, sib, edge,
    csem, ssem, rsem, essem, ersem,
):
    gz, gx = lax.axis_index("gz"), lax.axis_index("gx")
    row, core = gz // 2, gz % 2

    def at(chip_row, which, column):
        return lax.rem((chip_row + 32) * 2 + which, 32), lax.rem(column + 8, 8)

    other = 1 - core
    barrier = pltpu.get_barrier_semaphore()
    sources = [at(row, other, gx), at(row, 1, gx - 1), at(row, 0, gx + 1)]
    for ahead in (1, 2):
        sources += [at(row + ahead, which, gx) for which in (0, 1)]
    for source in sources:
        pl.semaphore_signal(barrier, inc=1, device_id=source, device_id_type=MESH)

    loads = [
        pltpu.make_async_copy(a, b, csem.at[i])
        for i, (a, b) in enumerate([(fz_hbm, fz), (fx_hbm, fx), (iz_hbm, iz), (ix_hbm, ix)])
    ]
    for load in loads:
        load.start()
    mine = pltpu.make_async_copy(
        dens.at[:, pl.ds(pl.multiple_of(core * 256, 256), 256)],
        win.at[pl.ds(pl.multiple_of(core * 128, 128), 128)],
        csem.at[4],
    )
    mine.start()
    pl.semaphore_wait(barrier, len(sources))

    def piece(behind, which, slot):
        return pltpu.make_async_remote_copy(
            src_ref=dens.at[:, pl.ds(pl.multiple_of(which * 256, 256), 256)],
            dst_ref=win.at[pl.ds(pl.multiple_of(behind * 256 + core * 128, 128), 128)],
            send_sem=ssem.at[slot],
            recv_sem=rsem.at[behind * 2 + core],
            device_id=at(row - behind, which, gx),
            device_id_type=MESH,
        )

    def arrived(ahead, which):
        here = win.at[pl.ds(pl.multiple_of(ahead * 256 + which * 128, 128), 128)]
        pltpu.make_async_remote_copy(
            src_ref=here, dst_ref=here, send_sem=ssem.at[0], recv_sem=rsem.at[ahead * 2 + which],
            device_id=at(row, other, gx), device_id_type=MESH,
        ).wait_recv()

    sends = [piece(1, 0, 0), piece(1, 1, 1), piece(2, 0, 2), piece(2, 1, 3), piece(0, other, 4)]
    for send in sends:
        send.start()

    for load in loads:
        load.wait()
    th, tl = split(zt_ref[...])
    for t in range(3):
        rows = slice(256 * t, 256 * t + 256)
        zt[rows, :] = dot3(fz[0, rows, :512], fz[1, rows, :512], th, tl, ((1,), (1,)))
    eh, el = split(xt_ref[...])
    sign = jnp.where(lax.broadcasted_iota(jnp.int32, (1, 512), 1) % 2 == 0, -NORM, NORM)
    eh, el = split(dot3(eh, el, fx[0], fx[1]) * sign)
    for t in range(3):
        rows = slice(256 * t, 256 * t + 256)
        zh, zl = split(zt[rows, :])
        khat[rows, :] = dot3(zh, zl, eh, el)

    mine.wait()
    for ahead in range(3):
        if ahead == 0:
            arrived(0, other)
        else:
            arrived(ahead, 0)
            arrived(ahead, 1)
        block = win[256 * ahead : 256 * ahead + 256, :]
        if ahead:
            block = jnp.where(row + ahead < 16, block, 0.0)
        bh, bl = split(block)
        for t in range(3):
            rows, cols = slice(256 * t, 256 * t + 256), slice(256 * ahead, 256 * ahead + 256)
            part = dot3(fz[0, rows, cols], fz[1, rows, cols], bh, bl)
            acc[rows, :] = part if ahead == 0 else acc[rows, :] + part

    for t in range(3):
        rows = slice(256 * t, 256 * t + 256)
        ah, al = split(acc[rows, :])
        d = dot3(ah, al, fx[0], fx[1])
        k = khat[rows, :]
        d0, d1, d2, d3 = d[:128, :256], d[128:, :256], d[:128, 256:], d[128:, 256:]
        k0, k1, k2, k3 = k[:128, 256:], k[128:, 256:], k[:128, :256], k[128:, :256]
        for r, c, value in (
            (0, 0, d0 * k0 + d1 * k1 - d2 * k2 - d3 * k3),
            (128, 0, d1 * k0 - d0 * k1 + d2 * k3 - d3 * k2),
            (0, 256, d0 * k2 + d2 * k0 + d1 * k3 + d3 * k1),
            (128, 256, d3 * k0 - d0 * k3 + d1 * k2 - d2 * k1),
        ):
            high, low = split(value)
            what[0, 256 * t + r : 256 * t + r + 128, c : c + 256] = high
            what[1, 256 * t + r : 256 * t + r + 128, c : c + 256] = low

    yh, yl = split(dot3(iz[0], iz[1], what[0], what[1]))
    wake[...] = dot3(yh, yl, ix[0], ix[1])

    own_from, own_to = pl.multiple_of(128 * other, 128), pl.multiple_of(128 * core, 128)
    step = 2 * core - 1
    gives = [
        pltpu.make_async_remote_copy(
            src_ref=wake.at[pl.ds(128 * r, 128), pl.ds(pl.multiple_of(384 * core, 128), 128)],
            dst_ref=edge.at[other], send_sem=essem.at[r], recv_sem=ersem.at[other],
            device_id=at(row, r, gx + step), device_id_type=MESH,
        )
        for r in (0, 1)
    ]
    gives.append(
        pltpu.make_async_remote_copy(
            src_ref=wake.at[pl.ds(pl.multiple_of(128 * other, 128), 128), pl.ds(own_from, 384)],
            dst_ref=sib, send_sem=essem.at[2], recv_sem=ersem.at[2],
            device_id=at(row, other, gx), device_id_type=MESH,
        )
    )
    for give in gives:
        give.start()
    rows = pl.ds(pl.multiple_of(128 * core, 128), 128)
    out[:, pl.ds(pl.multiple_of(384 * other, 128), 128)] = jnp.zeros((128, 128), F32)
    out[:, pl.ds(own_to, 384)] = wake[rows, pl.ds(own_from, 384)]
    gives[2].wait_recv()
    their = pl.ds(pl.multiple_of(128 * other, 128), 384)
    out[:, their] = out[:, their] + sib[...]
    for side in (0, 1):
        here = edge.at[side]
        pltpu.make_async_remote_copy(
            src_ref=here, dst_ref=here, send_sem=essem.at[0], recv_sem=ersem.at[side],
            device_id=at(row, other, gx), device_id_type=MESH,
        ).wait_recv()
        there = slice(0, 128) if side == 0 else slice(384, 512)
        inside = gx > 0 if side == 0 else gx < 7
        out[:, there] = out[:, there] + jnp.where(inside, edge[side], 0.0)
    for copy in sends + gives:
        copy.wait_send()


def local(mats, density, ztaps, xtaps):
    any_, vmem = pl.BlockSpec(memory_space=pl.ANY), pl.BlockSpec(memory_space=pltpu.VMEM)
    return pl.pallas_call(
        kernel,
        out_shape=jax.ShapeDtypeStruct(density.shape, F32),
        in_specs=[any_, vmem, vmem] + [any_] * 4,
        out_specs=vmem,
        scratch_shapes=[
            pltpu.VMEM((LZ, 256), F32),
            *[pltpu.VMEM(m.shape, BF16) for m in mats],
            pltpu.VMEM((LZ, 256), F32),
            pltpu.VMEM((LZ, LX), F32),
            pltpu.VMEM((LZ, 32), F32),
            pltpu.VMEM((2, LZ, LX), BF16),
            pltpu.VMEM((256, LX), F32),
            pltpu.VMEM((128, 384), F32),
            pltpu.VMEM((2, 128, 128), F32),
            pltpu.SemaphoreType.DMA((5,)),
            pltpu.SemaphoreType.DMA((5,)),
            pltpu.SemaphoreType.DMA((6,)),
            pltpu.SemaphoreType.DMA((3,)),
            pltpu.SemaphoreType.DMA((3,)),
        ],
        compiler_params=pltpu.CompilerParams(
            collective_id=0, has_side_effects=True, vmem_limit_bytes=48 * 2**20
        ),
    )(density, ztaps, xtaps, *mats)


def solution(mesh):
    mats = [jnp.asarray(m) for m in constants()]
    return jax.shard_map(
        lambda *args: local(mats, *args),
        mesh=mesh,
        in_specs=(P("gz", "gx"), P(), P()),
        out_specs=P("gz", "gx"),
        check_vma=False,
    )
```

profile of v0, /device:TPU:1, one launch (start us, length us, event | category | flops | bytes accessed | tf_op | source)
XLA Modules:
  0.0 45.2 jit_solution(6738126323441992652)
XLA Ops:
  0.0 0.0 copy-start
  0.0 1.7 %copy-done = bf16[2,768,768]{2,1,0:T(8,128)(2,1)S(1)} copy-done((bf16[2,768,768]{2,1,0:T(8,128)(2,1)S(1)}, bf16[2,768,768]{2,1,0:T(8,128)(2,1)}, u32[]{:S(2)}) %copy-start) | copy-done | bytes 2359320
  1.7 0.0 copy-start.1
  1.7 1.2 %copy-done.1 = bf16[2,512,512]{2,1,0:T(8,128)(2,1)S(1)} copy-done((bf16[2,512,512]{2,1,0:T(8,128)(2,1)S(1)}, bf16[2,512,512]{2,1,0:T(8,128)(2,1)}, u32[]{:S(2)}) %copy-start.1) | copy-done | bytes 1048600
  2.9 0.0 copy-start.2
  2.9 1.1 %copy-done.2 = bf16[2,256,768]{2,1,0:T(8,128)(2,1)S(1)} copy-done((bf16[2,256,768]{2,1,0:T(8,128)(2,1)S(1)}, bf16[2,256,768]{2,1,0:T(8,128)(2,1)}, u32[]{:S(2)}) %copy-start.2) | copy-done | bytes 786456
  4.0 0.0 copy-start.3
  4.0 1.0 %copy-done.3 = bf16[2,256,512]{2,1,0:T(8,128)(2,1)S(1)} copy-done((bf16[2,256,512]{2,1,0:T(8,128)(2,1)S(1)}, bf16[2,256,512]{2,1,0:T(8,128)(2,1)}, u32[]{:S(2)}) %copy-start.3) | copy-done | bytes 524312
  5.1 0.0 copy-start.4
  5.1 0.9 %copy-done.4 = f32[128,512]{1,0:T(8,128)S(1)} copy-done((f32[128,512]{1,0:T(8,128)S(1)}, f32[128,512]{1,0:T(8,128)}, u32[]{:S(2)}) %copy-start.4) | copy-done | bytes 262168
  6.0 0.0 copy-start.5
  6.0 0.8 %copy-done.5 = f32[32,512]{1,0:T(8,128)S(1)} copy-done((f32[32,512]{1,0:T(8,128)S(1)}, f32[32,512]{1,0:T(8,128)}, u32[]{:S(2)}) %copy-start.5) | copy-done | bytes 65560
  6.9 0.0 copy-start.6
  6.9 0.8 %copy-done.6 = f32[32,256]{1,0:T(8,128)S(1)} copy-done((f32[32,256]{1,0:T(8,128)S(1)}, f32[32,256]{1,0:T(8,128)}, u32[]{:S(2)}) %copy-start.6) | copy-done | bytes 32792
  7.6 36.8 %shard_map.73 = f32[128,512]{1,0:T(8,128)S(1)} custom-call(f32[128,512]{1,0:T(8,128)S(1)} %copy-done.4, f32[32,512]{1,0:T(8,128)S(1)} %copy-done.5, f32[32,256]{1,0:T(8,128)S(1)} %copy-done.6, bf16[2,768,768]{2,1,0:T(8,128)(2,1)S(1)} %copy-done, bf16[2,256,768]{2,1,0:T(8,128)(2,1)S(1)} %copy-done.2, bf16[2,256,512]{2,1,0:T(8,128)(2,1)S(1)} %copy-done.3, ...), custom_call_target="tpu_custom_call" | custom-call | tf_op jit(solution)/shard_map/pallas_call | solution.py:189
  44.5 0.7 %copy.9 = f32[128,512]{1,0:T(8,128)} copy(f32[128,512]{1,0:T(8,128)S(1)} %shard_map.73) | data formatting | bytes 524288
Async XLA Ops:
  0.0 1.7 %copy-start = (bf16[2,768,768]{2,1,0:T(8,128)(2,1)S(1)}, bf16[2,768,768]{2,1,0:T(8,128)(2,1)}, u32[]{:S(2)}) copy-start(bf16[2,768,768]{2,1,0:T(8,128)(2,1)} %constant.8.clone.fz_hbm) | copy-start | bytes 7077892
  1.7 1.2 %copy-start.1 = (bf16[2,512,512]{2,1,0:T(8,128)(2,1)S(1)}, bf16[2,512,512]{2,1,0:T(8,128)(2,1)}, u32[]{:S(2)}) copy-start(bf16[2,512,512]{2,1,0:T(8,128)(2,1)} %constant.11.clone.ix_hbm) | copy-start | bytes 3145732
  2.9 1.1 %copy-start.2 = (bf16[2,256,768]{2,1,0:T(8,128)(2,1)S(1)}, bf16[2,256,768]{2,1,0:T(8,128)(2,1)}, u32[]{:S(2)}) copy-start(bf16[2,256,768]{2,1,0:T(8,128)(2,1)} %constant.9.clone.iz_hbm) | copy-start | bytes 2359300
  4.0 1.0 %copy-start.3 = (bf16[2,256,512]{2,1,0:T(8,128)(2,1)S(1)}, bf16[2,256,512]{2,1,0:T(8,128)(2,1)}, u32[]{:S(2)}) copy-start(bf16[2,256,512]{2,1,0:T(8,128)(2,1)} %constant.10.clone.fx_hbm) | copy-start | bytes 1572868
  5.1 0.9 %copy-start.4 = (f32[128,512]{1,0:T(8,128)S(1)}, f32[128,512]{1,0:T(8,128)}, u32[]{:S(2)}) copy-start(f32[128,512]{1,0:T(8,128)} %dens.1) | copy-start | bytes 786436
  6.0 0.8 %copy-start.5 = (f32[32,512]{1,0:T(8,128)S(1)}, f32[32,512]{1,0:T(8,128)}, u32[]{:S(2)}) copy-start(f32[32,512]{1,0:T(8,128)} %zt_ref.1) | copy-start | bytes 196612
  6.9 0.8 %copy-start.6 = (f32[32,256]{1,0:T(8,128)S(1)}, f32[32,256]{1,0:T(8,128)}, u32[]{:S(2)}) copy-start(f32[32,256]{1,0:T(8,128)} %xt_ref.1) | copy-start | bytes 98308
where the time goes:
time: 45.5 us; the launch traced here: 45.2 us
  Pallas kernels  36.8 us (81%)
  local copies, waits for them, and re-layouts  8.31 us (18%)
    pallas_call x1, Pallas kernels, local(): pl.pallas_call(kernel, out_shape=jax.ShapeDtypeStruct(density.shape, F32)...  36.8 us
    unnamed x15, local copies, waits for them, and re-layouts  8.31 us

commit v1 on v0

--- a/solution.py
+++ b/solution.py
@@ -10,6 +10,7 @@
 MESH = pl.DeviceIdType.MESH
 F32, BF16 = jnp.float32, jnp.bfloat16
 LZ, LX = 768, 512
+CUT = 48
 NORM = 4.0 / (LZ * LX)
 
 
@@ -43,8 +44,8 @@
 
 
 def kernel(
-    dens, zt_ref, xt_ref, fz_hbm, iz_hbm, fx_hbm, ix_hbm, out,
-    win, fz, iz, fx, ix, acc, khat, zt, what, wake, sib, edge,
+    dens, zt_hbm, xt_hbm, fz_hbm, iz_hbm, fx_hbm, ix_hbm, out,
+    win, up_in, turn_in, zt_ref, xt_ref, fz, iz, fx, ix, acc, khat, zt, what, wake, sib, edge,
     csem, ssem, rsem, essem, ersem,
 ):
     gz, gx = lax.axis_index("gz"), lax.axis_index("gx")
@@ -53,48 +54,89 @@
     def at(chip_row, which, column):
         return lax.rem((chip_row + 32) * 2 + which, 32), lax.rem(column + 8, 8)
 
-    other = 1 - core
+    def along_y(chip_row, by):
+        chip_row = lax.rem(chip_row + 32, 16)
+        return chip_row // 4 * 4 + lax.rem(chip_row + 4 + by, 4)
+
+    other, last, first = 1 - core, row % 4 == 3, row % 4 == 0
     barrier = pltpu.get_barrier_semaphore()
     sources = [at(row, other, gx), at(row, 1, gx - 1), at(row, 0, gx + 1)]
-    for ahead in (1, 2):
-        sources += [at(row + ahead, which, gx) for which in (0, 1)]
+    sources += [at(along_y(row + 2, 1), core, gx), at(row + 4, core, gx)]
+    for which in (0, 1):
+        sources += [at(row + 1, which, gx), at(along_y(row, 1), which, gx), at(along_y(row, -1), which, gx)]
     for source in sources:
         pl.semaphore_signal(barrier, inc=1, device_id=source, device_id_type=MESH)
 
     loads = [
         pltpu.make_async_copy(a, b, csem.at[i])
-        for i, (a, b) in enumerate([(fz_hbm, fz), (fx_hbm, fx), (iz_hbm, iz), (ix_hbm, ix)])
+        for i, (a, b) in enumerate([(zt_hbm, zt_ref), (xt_hbm, xt_ref), (fz_hbm, fz), (fx_hbm, fx), (iz_hbm, iz), (ix_hbm, ix)])
     ]
     for load in loads:
         load.start()
     mine = pltpu.make_async_copy(
         dens.at[:, pl.ds(pl.multiple_of(core * 256, 256), 256)],
         win.at[pl.ds(pl.multiple_of(core * 128, 128), 128)],
-        csem.at[4],
+        csem.at[6],
     )
     mine.start()
     pl.semaphore_wait(barrier, len(sources))
 
-    def piece(behind, which, slot):
+    def half(which, start, stop):
+        return dens.at[start:stop, pl.ds(pl.multiple_of(which * 256, 256), 256)]
+
+    def rows_of(ahead, which, start, stop):
+        return win.at[pl.ds(pl.multiple_of(ahead * 256 + which * 128 + start, 16), stop - start)]
+
+    def send(source, there, slot, landing, device):
         return pltpu.make_async_remote_copy(
-            src_ref=dens.at[:, pl.ds(pl.multiple_of(which * 256, 256), 256)],
-            dst_ref=win.at[pl.ds(pl.multiple_of(behind * 256 + core * 128, 128), 128)],
-            send_sem=ssem.at[slot],
-            recv_sem=rsem.at[behind * 2 + core],
-            device_id=at(row - behind, which, gx),
-            device_id_type=MESH,
+            src_ref=source, dst_ref=there, send_sem=ssem.at[slot], recv_sem=rsem.at[landing],
+            device_id=device, device_id_type=MESH,
         )
 
-    def arrived(ahead, which):
-        here = win.at[pl.ds(pl.multiple_of(ahead * 256 + which * 128, 128), 128)]
-        pltpu.make_async_remote_copy(
-            src_ref=here, dst_ref=here, send_sem=ssem.at[0], recv_sem=rsem.at[ahead * 2 + which],
-            device_id=at(row, other, gx), device_id_type=MESH,
-        ).wait_recv()
-
-    sends = [piece(1, 0, 0), piece(1, 1, 1), piece(2, 0, 2), piece(2, 1, 3), piece(0, other, 4)]
-    for send in sends:
-        send.start()
+    def arrived(here, landing):
+        send(here, here, 0, landing, at(row, other, gx)).wait_recv()
+
+    sends = []
+    for which in (0, 1):
+        near = send(half(which, 0, CUT), rows_of(1, core, 0, CUT), which, core, at(row - 1, which, gx))
+        up = send(half(which, CUT, 128), up_in.at[core], 4 + which, 8 + core, at(along_y(row, 1), which, gx))
+        far = send(half(which, CUT, 128), rows_of(1, core, CUT, 128), 2 + which, 2 + core, at(row - 1, which, gx))
+        turn = send(half(which, CUT, 128), turn_in.at[core], 2 + which, 10 + core, at(along_y(row, -1), which, gx))
+        up.start()
+        pl.when(first)(turn.start)
+        pl.when(jnp.logical_not(first))(far.start)
+        near.start()
+        sends += [near, up, far]
+    sib_send = send(half(other, 0, 128), rows_of(0, core, 0, 128), 6, 12, at(row, other, gx))
+    sib_send.start()
+    sends.append(sib_send)
+
+    def relays():
+        passed, turned = [], []
+        for which in (0, 1):
+            arrived(up_in.at[which], 8 + which)
+            passed.append(
+                send(up_in.at[which], rows_of(2, which, CUT, 128), 7 + which, 4 + which, at(along_y(row, -1) - 2, core, gx))
+            )
+            passed[-1].start()
+        for which in (0, 1):
+            turned.append(
+                send(turn_in.at[which], rows_of(1, which, CUT, 128), 11 + which, 2 + which, at(row - 4, core, gx))
+            )
+
+        @pl.when(last)
+        def _():
+            for which in (0, 1):
+                arrived(turn_in.at[which], 10 + which)
+                turned[which].start()
+
+        for which in (0, 1):
+            arrived(rows_of(1, which, 0, CUT), which)
+            passed.append(
+                send(rows_of(1, which, 0, CUT), rows_of(2, which, 0, CUT), 9 + which, 6 + which, at(row - 1, core, gx))
+            )
+            passed[-1].start()
+        return passed, turned
 
     for load in loads:
         load.wait()
@@ -111,12 +153,15 @@
         khat[rows, :] = dot3(zh, zl, eh, el)
 
     mine.wait()
+    passed, turned = relays()
     for ahead in range(3):
         if ahead == 0:
-            arrived(0, other)
-        else:
-            arrived(ahead, 0)
-            arrived(ahead, 1)
+            arrived(rows_of(0, other, 0, 128), 12)
+        for which in (0, 1):
+            if ahead:
+                arrived(rows_of(ahead, which, CUT, 128), 2 * ahead + which)
+            if ahead == 2:
+                arrived(rows_of(2, which, 0, CUT), 6 + which)
         block = win[256 * ahead : 256 * ahead + 256, :]
         if ahead:
             block = jnp.where(row + ahead < 16, block, 0.0)
@@ -180,19 +225,25 @@
         there = slice(0, 128) if side == 0 else slice(384, 512)
         inside = gx > 0 if side == 0 else gx < 7
         out[:, there] = out[:, there] + jnp.where(inside, edge[side], 0.0)
-    for copy in sends + gives:
+    for copy in sends + passed + gives:
         copy.wait_send()
+    for copy in turned:
+        pl.when(last)(copy.wait_send)
 
 
 def local(mats, density, ztaps, xtaps):
-    any_, vmem = pl.BlockSpec(memory_space=pl.ANY), pl.BlockSpec(memory_space=pltpu.VMEM)
+    hbm, vmem = pl.BlockSpec(memory_space=pltpu.HBM), pl.BlockSpec(memory_space=pltpu.VMEM)
     return pl.pallas_call(
         kernel,
         out_shape=jax.ShapeDtypeStruct(density.shape, F32),
-        in_specs=[any_, vmem, vmem] + [any_] * 4,
+        in_specs=[hbm] * 7,
         out_specs=vmem,
         scratch_shapes=[
             pltpu.VMEM((LZ, 256), F32),
+            pltpu.VMEM((2, 128 - CUT, 256), F32),
+            pltpu.VMEM((2, 128 - CUT, 256), F32),
+            pltpu.VMEM(ztaps.shape, F32),
+            pltpu.VMEM(xtaps.shape, F32),
             *[pltpu.VMEM(m.shape, BF16) for m in mats],
             pltpu.VMEM((LZ, 256), F32),
             pltpu.VMEM((LZ, LX), F32),
@@ -201,14 +252,14 @@
             pltpu.VMEM((256, LX), F32),
             pltpu.VMEM((128, 384), F32),
             pltpu.VMEM((2, 128, 128), F32),
-            pltpu.SemaphoreType.DMA((5,)),
-            pltpu.SemaphoreType.DMA((5,)),
-            pltpu.SemaphoreType.DMA((6,)),
+            pltpu.SemaphoreType.DMA((7,)),
+            pltpu.SemaphoreType.DMA((13,)),
+            pltpu.SemaphoreType.DMA((13,)),
             pltpu.SemaphoreType.DMA((3,)),
             pltpu.SemaphoreType.DMA((3,)),
         ],
         compiler_params=pltpu.CompilerParams(
-            collective_id=0, has_side_effects=True, vmem_limit_bytes=48 * 2**20
+            collective_id=0, has_side_effects=True, vmem_limit_bytes=56 * 2**20
         ),
     )(density, ztaps, xtaps, *mats)
 

time: 45.5 us -> 33.6 us (0.74)
  the two profiles are of different devices: /device:TPU:1 before, /device:TPU:89 now
where the time goes in v1:
time: 33.6 us; the launch traced here: 33.5 us
  Pallas kernels  31.8 us (95%)
  local copies, waits for them, and re-layouts  1.67 us (5%)
    pallas_call x1, Pallas kernels, local(): pl.pallas_call(kernel, out_shape=jax.ShapeDtypeStruct(density.shape, F32)...  31.8 us
    unnamed x1, local copies, waits for them, and re-layouts  1.67 us

profile of v1, /device:TPU:89, one launch (start us, length us, event | category | flops | bytes accessed | tf_op | source)
XLA Modules:
  0.0 33.5 jit_solution(6262398644115331104)
XLA Ops:
  0.0 31.8 %shard_map.73 = f32[128,512]{1,0:T(8,128)} custom-call(f32[128,512]{1,0:T(8,128)} %dens.1, f32[32,512]{1,0:T(8,128)} %zt_hbm.1, f32[32,256]{1,0:T(8,128)} %xt_hbm.1, bf16[2,768,768]{2,1,0:T(8,128)(2,1)} %constant.8.clone.fz_hbm, bf16[2,256,768]{2,1,0:T(8,128)(2,1)} %constant.9.clone.iz_hbm, bf16[2,256,512]{2,1,0:T(8,128)(2,1)} %constant.10.clone.fx_hbm, ...), custom_call_target="tpu_custom_call" | custom-call | tf_op jit(solution)/shard_map/pallas_call | solution.py:236
  31.8 1.7 %copy.9 = f32[128,512]{1,0:T(8,128)} copy(f32[128,512]{1,0:T(8,128)} %shard_map.73) | data formatting | bytes 524288

commit v2 on v1

--- a/solution.py
+++ b/solution.py
@@ -1,3 +1,5 @@
+import functools
+
 import jax
 import jax.numpy as jnp
 import ml_dtypes
@@ -59,13 +61,32 @@
         return chip_row // 4 * 4 + lax.rem(chip_row + 4 + by, 4)
 
     other, last, first = 1 - core, row % 4 == 3, row % 4 == 0
+    up_row, step = along_y(row, -1), 2 * core - 1
+    sends_one, sends_two, passes = row >= 1, row >= 2, up_row >= 2
+    gets_one, gets_two = row <= 14, row <= 13
+    turns, gets_turned = last & (row > 3), last & (row <= 11)
+    gives_edge = (gx + step >= 0) & (gx + step <= 7)
     barrier = pltpu.get_barrier_semaphore()
-    sources = [at(row, other, gx), at(row, 1, gx - 1), at(row, 0, gx + 1)]
-    sources += [at(along_y(row + 2, 1), core, gx), at(row + 4, core, gx)]
-    for which in (0, 1):
-        sources += [at(row + 1, which, gx), at(along_y(row, 1), which, gx), at(along_y(row, -1), which, gx)]
-    for source in sources:
-        pl.semaphore_signal(barrier, inc=1, device_id=source, device_id_type=MESH)
+
+    def greet(when, *sources):
+        @pl.when(when)
+        def _():
+            for source in sources:
+                pl.semaphore_signal(barrier, inc=1, device_id=source, device_id_type=MESH)
+
+    pl.semaphore_signal(barrier, inc=1, device_id=at(row, other, gx), device_id_type=MESH)
+    greet(gets_one, *[at(row + 1, which, gx) for which in (0, 1)])
+    greet(gets_two, at(along_y(row + 2, 1), core, gx))
+    greet(passes, *[at(up_row, which, gx) for which in (0, 1)])
+    greet(turns, *[at(along_y(row, 1), which, gx) for which in (0, 1)])
+    greet(gets_turned, at(row + 4, core, gx))
+    greet(gx > 0, at(row, 1, gx - 1))
+    greet(gx < 7, at(row, 0, gx + 1))
+    greeted = 1
+    for when, number in (
+        (sends_one, 2), (passes, 1), (sends_two, 2), (first & sends_one, 2), (turns, 1), (gives_edge, 2)
+    ):
+        greeted = greeted + jnp.where(when, number, 0)
 
     loads = [
         pltpu.make_async_copy(a, b, csem.at[i])
@@ -79,7 +100,7 @@
         csem.at[6],
     )
     mine.start()
-    pl.semaphore_wait(barrier, len(sources))
+    pl.semaphore_wait(barrier, greeted)
 
     def half(which, start, stop):
         return dens.at[start:stop, pl.ds(pl.multiple_of(which * 256, 256), 256)]
@@ -102,41 +123,41 @@
         up = send(half(which, CUT, 128), up_in.at[core], 4 + which, 8 + core, at(along_y(row, 1), which, gx))
         far = send(half(which, CUT, 128), rows_of(1, core, CUT, 128), 2 + which, 2 + core, at(row - 1, which, gx))
         turn = send(half(which, CUT, 128), turn_in.at[core], 2 + which, 10 + core, at(along_y(row, -1), which, gx))
-        up.start()
-        pl.when(first)(turn.start)
-        pl.when(jnp.logical_not(first))(far.start)
-        near.start()
-        sends += [near, up, far]
+        pl.when(sends_two)(up.start)
+        pl.when(sends_one & first)(turn.start)
+        pl.when(sends_one & jnp.logical_not(first))(far.start)
+        pl.when(sends_one)(near.start)
+        sends += [(near, sends_one), (up, sends_two), (far, sends_one)]
     sib_send = send(half(other, 0, 128), rows_of(0, core, 0, 128), 6, 12, at(row, other, gx))
     sib_send.start()
-    sends.append(sib_send)
 
     def relays():
-        passed, turned = [], []
+        copies = []
         for which in (0, 1):
-            arrived(up_in.at[which], 8 + which)
-            passed.append(
-                send(up_in.at[which], rows_of(2, which, CUT, 128), 7 + which, 4 + which, at(along_y(row, -1) - 2, core, gx))
-            )
-            passed[-1].start()
-        for which in (0, 1):
-            turned.append(
-                send(turn_in.at[which], rows_of(1, which, CUT, 128), 11 + which, 2 + which, at(row - 4, core, gx))
-            )
-
-        @pl.when(last)
+            up = send(up_in.at[which], rows_of(2, which, CUT, 128), 7 + which, 4 + which, at(up_row - 2, core, gx))
+            turned = send(turn_in.at[which], rows_of(1, which, CUT, 128), 11 + which, 2 + which, at(row - 4, core, gx))
+            near = send(rows_of(1, which, 0, CUT), rows_of(2, which, 0, CUT), 9 + which, 6 + which, at(row - 1, core, gx))
+            copies += [(up, passes), (turned, turns), (near, sends_one & gets_one)]
+
+        @pl.when(passes)
+        def _():
+            for which in (0, 1):
+                arrived(up_in.at[which], 8 + which)
+                copies[3 * which][0].start()
+
+        @pl.when(turns)
         def _():
             for which in (0, 1):
                 arrived(turn_in.at[which], 10 + which)
-                turned[which].start()
-
-        for which in (0, 1):
-            arrived(rows_of(1, which, 0, CUT), which)
-            passed.append(
-                send(rows_of(1, which, 0, CUT), rows_of(2, which, 0, CUT), 9 + which, 6 + which, at(row - 1, core, gx))
-            )
-            passed[-1].start()
-        return passed, turned
+                copies[3 * which + 1][0].start()
+
+        @pl.when(gets_one)
+        def _():
+            for which in (0, 1):
+                arrived(rows_of(1, which, 0, CUT), which)
+                pl.when(sends_one)(copies[3 * which + 2][0].start)
+
+        return copies
 
     for load in loads:
         load.wait()
@@ -153,8 +174,9 @@
         khat[rows, :] = dot3(zh, zl, eh, el)
 
     mine.wait()
-    passed, turned = relays()
-    for ahead in range(3):
+    passed = relays()
+
+    def add_block(ahead):
         if ahead == 0:
             arrived(rows_of(0, other, 0, 128), 12)
         for which in (0, 1):
@@ -162,14 +184,15 @@
                 arrived(rows_of(ahead, which, CUT, 128), 2 * ahead + which)
             if ahead == 2:
                 arrived(rows_of(2, which, 0, CUT), 6 + which)
-        block = win[256 * ahead : 256 * ahead + 256, :]
-        if ahead:
-            block = jnp.where(row + ahead < 16, block, 0.0)
-        bh, bl = split(block)
+        bh, bl = split(win[256 * ahead : 256 * ahead + 256, :])
         for t in range(3):
             rows, cols = slice(256 * t, 256 * t + 256), slice(256 * ahead, 256 * ahead + 256)
             part = dot3(fz[0, rows, cols], fz[1, rows, cols], bh, bl)
             acc[rows, :] = part if ahead == 0 else acc[rows, :] + part
+
+    add_block(0)
+    pl.when(gets_one)(functools.partial(add_block, 1))
+    pl.when(gets_two)(functools.partial(add_block, 2))
 
     for t in range(3):
         rows = slice(256 * t, 256 * t + 256)
@@ -192,7 +215,6 @@
     wake[...] = dot3(yh, yl, ix[0], ix[1])
 
     own_from, own_to = pl.multiple_of(128 * other, 128), pl.multiple_of(128 * core, 128)
-    step = 2 * core - 1
     gives = [
         pltpu.make_async_remote_copy(
             src_ref=wake.at[pl.ds(128 * r, 128), pl.ds(pl.multiple_of(384 * core, 128), 128)],
@@ -201,34 +223,39 @@
         )
         for r in (0, 1)
     ]
-    gives.append(
+    gives = [(give, gives_edge) for give in gives]
+    across = (
         pltpu.make_async_remote_copy(
             src_ref=wake.at[pl.ds(pl.multiple_of(128 * other, 128), 128), pl.ds(own_from, 384)],
             dst_ref=sib, send_sem=essem.at[2], recv_sem=ersem.at[2],
             device_id=at(row, other, gx), device_id_type=MESH,
         )
     )
-    for give in gives:
-        give.start()
+    for give, when in gives:
+        pl.when(when)(give.start)
+    across.start()
     rows = pl.ds(pl.multiple_of(128 * core, 128), 128)
     out[:, pl.ds(pl.multiple_of(384 * other, 128), 128)] = jnp.zeros((128, 128), F32)
     out[:, pl.ds(own_to, 384)] = wake[rows, pl.ds(own_from, 384)]
-    gives[2].wait_recv()
+    across.wait_recv()
     their = pl.ds(pl.multiple_of(128 * other, 128), 384)
     out[:, their] = out[:, their] + sib[...]
-    for side in (0, 1):
+
+    def add_edge(side):
         here = edge.at[side]
         pltpu.make_async_remote_copy(
             src_ref=here, dst_ref=here, send_sem=essem.at[0], recv_sem=ersem.at[side],
             device_id=at(row, other, gx), device_id_type=MESH,
         ).wait_recv()
         there = slice(0, 128) if side == 0 else slice(384, 512)
-        inside = gx > 0 if side == 0 else gx < 7
-        out[:, there] = out[:, there] + jnp.where(inside, edge[side], 0.0)
-    for copy in sends + passed + gives:
-        copy.wait_send()
-    for copy in turned:
-        pl.when(last)(copy.wait_send)
+        out[:, there] = out[:, there] + edge[side]
+
+    pl.when(gx > 0)(functools.partial(add_edge, 0))
+    pl.when(gx < 7)(functools.partial(add_edge, 1))
+    sib_send.wait_send()
+    across.wait_send()
+    for copy, when in sends + passed + gives:
+        pl.when(when)(copy.wait_send)
 
 
 def local(mats, density, ztaps, xtaps):

time: 33.6 us -> 30.7 us (0.914)
  the two profiles are of different devices: /device:TPU:89 before, /device:TPU:95 now
where the time goes in v2:
time: 30.7 us; the launch traced here: 30.6 us
  Pallas kernels  28.9 us (94%)
  local copies, waits for them, and re-layouts  1.67 us (5%)
    pallas_call x1, Pallas kernels, local(): pl.pallas_call(kernel, out_shape=jax.ShapeDtypeStruct(density.shape, F32)...  28.9 us
    unnamed x1, local copies, waits for them, and re-layouts  1.67 us

profile of v2, /device:TPU:95, one launch (start us, length us, event | category | flops | bytes accessed | tf_op | source)
XLA Modules:
  0.0 30.6 jit_solution(10085627127390499317)
XLA Ops:
  0.0 28.9 %shard_map.73 = f32[128,512]{1,0:T(8,128)} custom-call(f32[128,512]{1,0:T(8,128)} %dens.1, f32[32,512]{1,0:T(8,128)} %zt_hbm.1, f32[32,256]{1,0:T(8,128)} %xt_hbm.1, bf16[2,768,768]{2,1,0:T(8,128)(2,1)} %constant.8.clone.fz_hbm, bf16[2,256,768]{2,1,0:T(8,128)(2,1)} %constant.9.clone.iz_hbm, bf16[2,256,512]{2,1,0:T(8,128)(2,1)} %constant.10.clone.fx_hbm, ...), custom_call_target="tpu_custom_call" | custom-call | tf_op jit(solution)/shard_map/pallas_call | solution.py:263
  28.9 1.7 %copy.9 = f32[128,512]{1,0:T(8,128)} copy(f32[128,512]{1,0:T(8,128)} %shard_map.73) | data formatting | bytes 524288

commit v3 on v2

--- a/solution.py
+++ b/solution.py
@@ -12,7 +12,8 @@
 MESH = pl.DeviceIdType.MESH
 F32, BF16 = jnp.float32, jnp.bfloat16
 LZ, LX = 768, 512
-CUT = 48
+CUT = 64
+PARTS = 1
 NORM = 4.0 / (LZ * LX)
 
 
@@ -117,45 +118,81 @@
     def arrived(here, landing):
         send(here, here, 0, landing, at(row, other, gx)).wait_recv()
 
+    def landing(kind, which, part):
+        return (kind * 2 + which) * PARTS + part
+
+    def near_rows(part):
+        return CUT // PARTS * part, CUT // PARTS * (part + 1)
+
+    def far_rows(part):
+        return tuple(CUT + (128 - CUT) // PARTS * (part + i) for i in (0, 1))
+
+    slots = iter(range(16 * PARTS))
     sends = []
-    for which in (0, 1):
-        near = send(half(which, 0, CUT), rows_of(1, core, 0, CUT), which, core, at(row - 1, which, gx))
-        up = send(half(which, CUT, 128), up_in.at[core], 4 + which, 8 + core, at(along_y(row, 1), which, gx))
-        far = send(half(which, CUT, 128), rows_of(1, core, CUT, 128), 2 + which, 2 + core, at(row - 1, which, gx))
-        turn = send(half(which, CUT, 128), turn_in.at[core], 2 + which, 10 + core, at(along_y(row, -1), which, gx))
-        pl.when(sends_two)(up.start)
-        pl.when(sends_one & first)(turn.start)
-        pl.when(sends_one & jnp.logical_not(first))(far.start)
-        pl.when(sends_one)(near.start)
-        sends += [(near, sends_one), (up, sends_two), (far, sends_one)]
-    sib_send = send(half(other, 0, 128), rows_of(0, core, 0, 128), 6, 12, at(row, other, gx))
+    for part in range(PARTS):
+        for which in (0, 1):
+            slot = next(slots)
+            up = send(
+                half(which, *far_rows(part)), up_in.at[core, part], next(slots), landing(4, core, part),
+                at(along_y(row, 1), which, gx),
+            )
+            far = send(
+                half(which, *far_rows(part)), rows_of(1, core, *far_rows(part)), slot, landing(1, core, part),
+                at(row - 1, which, gx),
+            )
+            turn = send(
+                half(which, *far_rows(part)), turn_in.at[core, part], slot, landing(5, core, part),
+                at(along_y(row, -1), which, gx),
+            )
+            near = send(
+                half(which, *near_rows(part)), rows_of(1, core, *near_rows(part)), next(slots), landing(0, core, part),
+                at(row - 1, which, gx),
+            )
+            pl.when(sends_two)(up.start)
+            pl.when(sends_one & first)(turn.start)
+            pl.when(sends_one & jnp.logical_not(first))(far.start)
+            pl.when(sends_one)(near.start)
+            sends += [(near, sends_one), (up, sends_two), (far, sends_one)]
+    sib_send = send(half(other, 0, 128), rows_of(0, core, 0, 128), next(slots), 12 * PARTS, at(row, other, gx))
     sib_send.start()
 
     def relays():
         copies = []
-        for which in (0, 1):
-            up = send(up_in.at[which], rows_of(2, which, CUT, 128), 7 + which, 4 + which, at(up_row - 2, core, gx))
-            turned = send(turn_in.at[which], rows_of(1, which, CUT, 128), 11 + which, 2 + which, at(row - 4, core, gx))
-            near = send(rows_of(1, which, 0, CUT), rows_of(2, which, 0, CUT), 9 + which, 6 + which, at(row - 1, core, gx))
-            copies += [(up, passes), (turned, turns), (near, sends_one & gets_one)]
-
-        @pl.when(passes)
-        def _():
+        for part in range(PARTS):
+            ups, turneds, nears = [], [], []
             for which in (0, 1):
-                arrived(up_in.at[which], 8 + which)
-                copies[3 * which][0].start()
-
-        @pl.when(turns)
-        def _():
-            for which in (0, 1):
-                arrived(turn_in.at[which], 10 + which)
-                copies[3 * which + 1][0].start()
-
-        @pl.when(gets_one)
-        def _():
-            for which in (0, 1):
-                arrived(rows_of(1, which, 0, CUT), which)
-                pl.when(sends_one)(copies[3 * which + 2][0].start)
+                ups.append(send(
+                    up_in.at[which, part], rows_of(2, which, *far_rows(part)), next(slots), landing(2, which, part),
+                    at(up_row - 2, core, gx),
+                ))
+                turneds.append(send(
+                    turn_in.at[which, part], rows_of(1, which, *far_rows(part)), next(slots), landing(1, which, part),
+                    at(row - 4, core, gx),
+                ))
+                nears.append(send(
+                    rows_of(1, which, *near_rows(part)), rows_of(2, which, *near_rows(part)), next(slots),
+                    landing(3, which, part), at(row - 1, core, gx),
+                ))
+            copies += [(c, passes) for c in ups] + [(c, turns) for c in turneds]
+            copies += [(c, sends_one & gets_one) for c in nears]
+
+            @pl.when(passes)
+            def _():
+                for which in (0, 1):
+                    arrived(up_in.at[which, part], landing(4, which, part))
+                    ups[which].start()
+
+            @pl.when(turns)
+            def _():
+                for which in (0, 1):
+                    arrived(turn_in.at[which, part], landing(5, which, part))
+                    turneds[which].start()
+
+            @pl.when(gets_one)
+            def _():
+                for which in (0, 1):
+                    arrived(rows_of(1, which, *near_rows(part)), landing(0, which, part))
+                    pl.when(sends_one)(nears[which].start)
 
         return copies
 
@@ -178,12 +215,12 @@
 
     def add_block(ahead):
         if ahead == 0:
-            arrived(rows_of(0, other, 0, 128), 12)
-        for which in (0, 1):
-            if ahead:
-                arrived(rows_of(ahead, which, CUT, 128), 2 * ahead + which)
-            if ahead == 2:
-                arrived(rows_of(2, which, 0, CUT), 6 + which)
+            arrived(rows_of(0, other, 0, 128), 12 * PARTS)
+        for part in range(PARTS if ahead else 0):
+            for which in (0, 1):
+                arrived(rows_of(ahead, which, *far_rows(part)), landing(ahead, which, part))
+                if ahead == 2:
+                    arrived(rows_of(2, which, *near_rows(part)), landing(3, which, part))
         bh, bl = split(win[256 * ahead : 256 * ahead + 256, :])
         for t in range(3):
             rows, cols = slice(256 * t, 256 * t + 256), slice(256 * ahead, 256 * ahead + 256)
@@ -267,8 +304,8 @@
         out_specs=vmem,
         scratch_shapes=[
             pltpu.VMEM((LZ, 256), F32),
-            pltpu.VMEM((2, 128 - CUT, 256), F32),
-            pltpu.VMEM((2, 128 - CUT, 256), F32),
+            pltpu.VMEM((2, PARTS, (128 - CUT) // PARTS, 256), F32),
+            pltpu.VMEM((2, PARTS, (128 - CUT) // PARTS, 256), F32),
             pltpu.VMEM(ztaps.shape, F32),
             pltpu.VMEM(xtaps.shape, F32),
             *[pltpu.VMEM(m.shape, BF16) for m in mats],
@@ -280,8 +317,8 @@
             pltpu.VMEM((128, 384), F32),
             pltpu.VMEM((2, 128, 128), F32),
             pltpu.SemaphoreType.DMA((7,)),
-            pltpu.SemaphoreType.DMA((13,)),
-            pltpu.SemaphoreType.DMA((13,)),
+            pltpu.SemaphoreType.DMA((16 * PARTS,)),
+            pltpu.SemaphoreType.DMA((12 * PARTS + 1,)),
             pltpu.SemaphoreType.DMA((3,)),
             pltpu.SemaphoreType.DMA((3,)),
         ],

time: 30.7 us -> 29 us (0.945)
  the two profiles are of different devices: /device:TPU:95 before, /device:TPU:115 now
where the time goes in v3:
time: 29 us; the launch traced here: 28.9 us
  Pallas kernels  27.2 us (94%)
  local copies, waits for them, and re-layouts  1.67 us (6%)
    pallas_call x1, Pallas kernels, local(): pl.pallas_call(kernel, out_shape=jax.ShapeDtypeStruct(density.shape, F32)...  27.2 us
    unnamed x1, local copies, waits for them, and re-layouts  1.67 us

profile of v3, /device:TPU:115, one launch (start us, length us, event | category | flops | bytes accessed | tf_op | source)
XLA Modules:
  0.0 28.9 jit_solution(9328043817626668273)
XLA Ops:
  0.0 27.2 %shard_map.73 = f32[128,512]{1,0:T(8,128)} custom-call(f32[128,512]{1,0:T(8,128)} %dens.1, f32[32,512]{1,0:T(8,128)} %zt_hbm.1, f32[32,256]{1,0:T(8,128)} %xt_hbm.1, bf16[2,768,768]{2,1,0:T(8,128)(2,1)} %constant.8.clone.fz_hbm, bf16[2,256,768]{2,1,0:T(8,128)(2,1)} %constant.9.clone.iz_hbm, bf16[2,256,512]{2,1,0:T(8,128)(2,1)} %constant.10.clone.fx_hbm, ...), custom_call_target="tpu_custom_call" | custom-call | tf_op jit(solution)/shard_map/pallas_call | solution.py:300
  27.2 1.7 %copy.9 = f32[128,512]{1,0:T(8,128)} copy(f32[128,512]{1,0:T(8,128)} %shard_map.73) | data formatting | bytes 524288

commit v4 on v3

--- a/solution.py
+++ b/solution.py
@@ -38,7 +38,8 @@
 
 
 def dot3(ah, al, bh, bl, dims=((1,), (0,))):
-    return dot(ah, bh, dims) + dot(ah, bl, dims) + dot(al, bh, dims)
+    axis = dims[1][0]
+    return dot(jnp.concatenate([ah, ah, al], axis=1), jnp.concatenate([bh, bl, bh], axis=axis), dims)
 
 
 def split(value):
@@ -248,29 +249,25 @@
             what[0, 256 * t + r : 256 * t + r + 128, c : c + 256] = high
             what[1, 256 * t + r : 256 * t + r + 128, c : c + 256] = low
 
-    yh, yl = split(dot3(iz[0], iz[1], what[0], what[1]))
-    wake[...] = dot3(yh, yl, ix[0], ix[1])
-
     own_from, own_to = pl.multiple_of(128 * other, 128), pl.multiple_of(128 * core, 128)
-    gives = [
-        pltpu.make_async_remote_copy(
+    across = pltpu.make_async_remote_copy(
+        src_ref=wake.at[pl.ds(pl.multiple_of(128 * other, 128), 128), pl.ds(own_from, 384)],
+        dst_ref=sib, send_sem=essem.at[2], recv_sem=ersem.at[2],
+        device_id=at(row, other, gx), device_id_type=MESH,
+    )
+    gives = []
+    for r in (0, 1):
+        rows = slice(128 * r, 128 * r + 128)
+        yh, yl = split(dot3(iz[0, rows, :], iz[1, rows, :], what[0], what[1]))
+        wake[rows, :] = dot3(yh, yl, ix[0], ix[1])
+        give = pltpu.make_async_remote_copy(
             src_ref=wake.at[pl.ds(128 * r, 128), pl.ds(pl.multiple_of(384 * core, 128), 128)],
             dst_ref=edge.at[other], send_sem=essem.at[r], recv_sem=ersem.at[other],
             device_id=at(row, r, gx + step), device_id_type=MESH,
         )
-        for r in (0, 1)
-    ]
-    gives = [(give, gives_edge) for give in gives]
-    across = (
-        pltpu.make_async_remote_copy(
-            src_ref=wake.at[pl.ds(pl.multiple_of(128 * other, 128), 128), pl.ds(own_from, 384)],
-            dst_ref=sib, send_sem=essem.at[2], recv_sem=ersem.at[2],
-            device_id=at(row, other, gx), device_id_type=MESH,
-        )
-    )
-    for give, when in gives:
-        pl.when(when)(give.start)
-    across.start()
+        pl.when(gives_edge)(give.start)
+        pl.when(other == r)(across.start)
+        gives.append((give, gives_edge))
     rows = pl.ds(pl.multiple_of(128 * core, 128), 128)
     out[:, pl.ds(pl.multiple_of(384 * other, 128), 128)] = jnp.zeros((128, 128), F32)
     out[:, pl.ds(own_to, 384)] = wake[rows, pl.ds(own_from, 384)]

time: 29 us -> 28.8 us (level)
  no operation moved by 1% of the time
where the time goes in v4:
time: 28.8 us; the launch traced here: 28.7 us
  Pallas kernels  27 us (94%)
  local copies, waits for them, and re-layouts  1.67 us (6%)
    pallas_call x1, Pallas kernels, local(): pl.pallas_call(kernel, out_shape=jax.ShapeDtypeStruct(density.shape, F32)...  27 us
    unnamed x1, local copies, waits for them, and re-layouts  1.67 us

profile of v4, /device:TPU:115, one launch (start us, length us, event | category | flops | bytes accessed | tf_op | source)
XLA Modules:
  0.0 28.7 jit_solution(15396933440918399990)
XLA Ops:
  0.0 27.0 %shard_map.73 = f32[128,512]{1,0:T(8,128)} custom-call(f32[128,512]{1,0:T(8,128)} %dens.1, f32[32,512]{1,0:T(8,128)} %zt_hbm.1, f32[32,256]{1,0:T(8,128)} %xt_hbm.1, bf16[2,768,768]{2,1,0:T(8,128)(2,1)} %constant.8.clone.fz_hbm, bf16[2,256,768]{2,1,0:T(8,128)(2,1)} %constant.9.clone.iz_hbm, bf16[2,256,512]{2,1,0:T(8,128)(2,1)} %constant.10.clone.fx_hbm, ...), custom_call_target="tpu_custom_call" | custom-call | tf_op jit(solution)/shard_map/pallas_call | solution.py:297
  27.0 1.7 %copy.9 = f32[128,512]{1,0:T(8,128)} copy(f32[128,512]{1,0:T(8,128)} %shard_map.73) | data formatting | bytes 524288

commit v5 on v4

--- a/solution.py
+++ b/solution.py
@@ -13,6 +13,7 @@
 F32, BF16 = jnp.float32, jnp.bfloat16
 LZ, LX = 768, 512
 CUT = 64
+TURN = 64
 PARTS = 1
 NORM = 4.0 / (LZ * LX)
 
@@ -122,11 +123,7 @@
     def landing(kind, which, part):
         return (kind * 2 + which) * PARTS + part
 
-    def near_rows(part):
-        return CUT // PARTS * part, CUT // PARTS * (part + 1)
-
-    def far_rows(part):
-        return tuple(CUT + (128 - CUT) // PARTS * (part + i) for i in (0, 1))
+    near_rows, far_rows, low_rows, high_rows = (0, TURN), (TURN, 128), (0, CUT), (CUT, 128)
 
     slots = iter(range(16 * PARTS))
     sends = []
@@ -134,19 +131,19 @@
         for which in (0, 1):
             slot = next(slots)
             up = send(
-                half(which, *far_rows(part)), up_in.at[core, part], next(slots), landing(4, core, part),
+                half(which, *high_rows), up_in.at[core, part], next(slots), landing(4, core, part),
                 at(along_y(row, 1), which, gx),
             )
             far = send(
-                half(which, *far_rows(part)), rows_of(1, core, *far_rows(part)), slot, landing(1, core, part),
+                half(which, *far_rows), rows_of(1, core, *far_rows), slot, landing(1, core, part),
                 at(row - 1, which, gx),
             )
             turn = send(
-                half(which, *far_rows(part)), turn_in.at[core, part], slot, landing(5, core, part),
+                half(which, *far_rows), turn_in.at[core, part], slot, landing(5, core, part),
                 at(along_y(row, -1), which, gx),
             )
             near = send(
-                half(which, *near_rows(part)), rows_of(1, core, *near_rows(part)), next(slots), landing(0, core, part),
+                half(which, *near_rows), rows_of(1, core, *near_rows), next(slots), landing(0, core, part),
                 at(row - 1, which, gx),
             )
             pl.when(sends_two)(up.start)
@@ -158,44 +155,47 @@
     sib_send.start()
 
     def relays():
-        copies = []
+        copies, steps = [], []
         for part in range(PARTS):
             ups, turneds, nears = [], [], []
             for which in (0, 1):
                 ups.append(send(
-                    up_in.at[which, part], rows_of(2, which, *far_rows(part)), next(slots), landing(2, which, part),
+                    up_in.at[which, part], rows_of(2, which, *high_rows), next(slots), landing(2, which, part),
                     at(up_row - 2, core, gx),
                 ))
                 turneds.append(send(
-                    turn_in.at[which, part], rows_of(1, which, *far_rows(part)), next(slots), landing(1, which, part),
+                    turn_in.at[which, part], rows_of(1, which, *far_rows), next(slots), landing(1, which, part),
                     at(row - 4, core, gx),
                 ))
                 nears.append(send(
-                    rows_of(1, which, *near_rows(part)), rows_of(2, which, *near_rows(part)), next(slots),
+                    rows_of(1, which, *low_rows), rows_of(2, which, *low_rows), next(slots),
                     landing(3, which, part), at(row - 1, core, gx),
                 ))
             copies += [(c, passes) for c in ups] + [(c, turns) for c in turneds]
             copies += [(c, sends_one & gets_one) for c in nears]
 
-            @pl.when(passes)
-            def _():
+            def relay_passes():
                 for which in (0, 1):
                     arrived(up_in.at[which, part], landing(4, which, part))
                     ups[which].start()
 
-            @pl.when(turns)
-            def _():
+            def relay_turns():
                 for which in (0, 1):
                     arrived(turn_in.at[which, part], landing(5, which, part))
                     turneds[which].start()
 
-            @pl.when(gets_one)
-            def _():
+            def relay_gets_one():
                 for which in (0, 1):
-                    arrived(rows_of(1, which, *near_rows(part)), landing(0, which, part))
+                    arrived(rows_of(1, which, *near_rows), landing(0, which, part))
                     pl.when(sends_one)(nears[which].start)
 
-        return copies
+            steps += [(passes, relay_passes), (turns, relay_turns), (gets_one, relay_gets_one)]
+        return copies, steps
+
+    passed, steps = relays()
+    relays_first = row >= 4
+    for when, relay in steps:
+        pl.when(relays_first & when)(relay)
 
     for load in loads:
         load.wait()
@@ -212,16 +212,17 @@
         khat[rows, :] = dot3(zh, zl, eh, el)
 
     mine.wait()
-    passed = relays()
+    for when, relay in steps:
+        pl.when(jnp.logical_not(relays_first) & when)(relay)
 
     def add_block(ahead):
         if ahead == 0:
             arrived(rows_of(0, other, 0, 128), 12 * PARTS)
         for part in range(PARTS if ahead else 0):
             for which in (0, 1):
-                arrived(rows_of(ahead, which, *far_rows(part)), landing(ahead, which, part))
+                arrived(rows_of(ahead, which, *(far_rows if ahead == 1 else high_rows)), landing(ahead, which, part))
                 if ahead == 2:
-                    arrived(rows_of(2, which, *near_rows(part)), landing(3, which, part))
+                    arrived(rows_of(2, which, *low_rows), landing(3, which, part))
         bh, bl = split(win[256 * ahead : 256 * ahead + 256, :])
         for t in range(3):
             rows, cols = slice(256 * t, 256 * t + 256), slice(256 * ahead, 256 * ahead + 256)
@@ -301,8 +302,8 @@
         out_specs=vmem,
         scratch_shapes=[
             pltpu.VMEM((LZ, 256), F32),
-            pltpu.VMEM((2, PARTS, (128 - CUT) // PARTS, 256), F32),
-            pltpu.VMEM((2, PARTS, (128 - CUT) // PARTS, 256), F32),
+            pltpu.VMEM((2, PARTS, 128 - CUT, 256), F32),
+            pltpu.VMEM((2, PARTS, 128 - TURN, 256), F32),
             pltpu.VMEM(ztaps.shape, F32),
             pltpu.VMEM(xtaps.shape, F32),
             *[pltpu.VMEM(m.shape, BF16) for m in mats],

time: 28.8 us -> 28.8 us (level)
  no operation moved by 1% of the time
where the time goes in v5:
time: 28.8 us; the launch traced here: 28.7 us
  Pallas kernels  27 us (94%)
  local copies, waits for them, and re-layouts  1.67 us (6%)
    pallas_call x1, Pallas kernels, local(): pl.pallas_call(kernel, out_shape=jax.ShapeDtypeStruct(density.shape, F32)...  27 us
    unnamed x1, local copies, waits for them, and re-layouts  1.67 us

profile of v5, /device:TPU:115, one launch (start us, length us, event | category | flops | bytes accessed | tf_op | source)
XLA Modules:
  0.0 28.7 jit_solution(8196833728850192232)
XLA Ops:
  0.0 27.0 %shard_map.73 = f32[128,512]{1,0:T(8,128)} custom-call(f32[128,512]{1,0:T(8,128)} %dens.1, f32[32,512]{1,0:T(8,128)} %zt_hbm.1, f32[32,256]{1,0:T(8,128)} %xt_hbm.1, bf16[2,768,768]{2,1,0:T(8,128)(2,1)} %constant.8.clone.fz_hbm, bf16[2,256,768]{2,1,0:T(8,128)(2,1)} %constant.9.clone.iz_hbm, bf16[2,256,512]{2,1,0:T(8,128)(2,1)} %constant.10.clone.fx_hbm, ...), custom_call_target="tpu_custom_call" | custom-call | tf_op jit(solution)/shard_map/pallas_call | solution.py:298
  27.0 1.7 %copy.9 = f32[128,512]{1,0:T(8,128)} copy(f32[128,512]{1,0:T(8,128)} %shard_map.73) | data formatting | bytes 524288
